TPU v7x, 768 devices: a whole 4x8x12 slice. The times are simulated.
768 devices in a mesh: node: 48 (over z_lo, y, core), orb: 16 (over x, z_hi).
Axes of the slice: x: 4, y: 8, z: 12 (z_hi: 4, z_lo: 3; z = z_hi * 3 + z_lo), core: 2. Of those that a mesh axis runs over, the one named last changes fastest.
Arguments:
- panel: bfloat16 [96, 64, 128, 128], P('node', 'orb'), may hold values from -6 to 6
- orbitals: bfloat16 [96, 64, 128, 256], P('node', 'orb'), may hold values from -6 to 6
- potential: float32 [96, 64, 128], P('node', 'orb'), may hold values from 0 to 2
- projectors: bfloat16 [18432, 256], P(('node', 'orb')), may hold values from -0.375 to 0.375
- strengths: bfloat16 [18432], P(('node', 'orb')), may hold values from 0.5 to 4
- atom_domain: int32 [18432, 1], P(('node', 'orb')), may hold values from 0 to 47; in each aligned block of 24 rows (0 to 23, 24 to 47, ...) at most 2 rows name the same one
- patch_start: int32 [18432], P(('node', 'orb')), may hold values from 0 to 768
Outputs:
- filtered_panel: bfloat16 [96, 64, 128, 128], P('node', 'orb')
- intersection: float32 [128, 256], replicated
Inputs may be any that keep to these rules, and one draw needn't show every extreme that they name: `atom_domain`: at most 2 of the 24 atoms held by one device name the same domain, and some device's atoms name one domain exactly 2 times.
All inputs are finite; a program needn't handle non-finite values.
Results may differ from a plain program's by a relative error of at most 0.009.
Values may be sent and summed in bfloat16 or wider, within the bound.
A program may use at most 32 MiB of HBM per device.

v0:
```python
import math

import jax
import jax.numpy as jnp
from jax import lax
from jax.sharding import PartitionSpec as P

DEG = 6


shift_point = 5.25
half_range = 3.25


def padded_2(block, sides, width):
    for axis, dim in sides:
        count = lax.axis_size(axis)
        forward = [(i, i + 1) for i in range(count - 1)]
        backward = [(target, source) for source, target in forward]
        low = lax.ppermute(
            lax.slice_in_dim(block, block.shape[dim] - width, None, axis=dim), axis, forward
        )
        high = lax.ppermute(lax.slice_in_dim(block, 0, width, axis=dim), axis, backward)
        block = jnp.concatenate([low, block, high], axis=dim)
    return block


def operate(extended, potential):
    padded = jnp.pad(extended.astype(jnp.float32), ((0, 0), (0, 0), (1, 1), (0, 0)))
    middle = padded[1:-1, 1:-1, 1:-1]
    neighbours = padded[2:, 1:-1, 1:-1] + padded[:-2, 1:-1, 1:-1]
    neighbours = neighbours + padded[1:-1, 2:, 1:-1] + padded[1:-1, :-2, 1:-1]
    neighbours = neighbours + padded[1:-1, 1:-1, 2:] + padded[1:-1, 1:-1, :-2]
    return (
        (3.0 + potential[..., None]) * middle - 0.5 * neighbours - shift_point * middle
    ) / half_range


def atom_part(values, scaled, starts, flat_panel, flat_orbit):
    slot_count, patch_len = values.shape
    col_index = starts[:, None] + jnp.arange(patch_len, dtype=jnp.int32)[None, :]
    row_index = jnp.broadcast_to(jnp.arange(slot_count, dtype=jnp.int32)[:, None], col_index.shape)
    weights = (
        jnp.zeros((slot_count, flat_panel.shape[0]), jnp.bfloat16)
        .at[row_index, col_index]
        .set(values)
    )
    panel_proj = (
        jnp.dot(weights, flat_panel, preferred_element_type=jnp.float32)
        * scaled.astype(jnp.float32)[:, None]
    )
    orbit_proj = jnp.dot(weights, flat_orbit, preferred_element_type=jnp.float32)
    return lax.dot_general(
        panel_proj,
        orbit_proj,
        (((0,), (0,)), ((), ())),
        precision=lax.Precision.HIGHEST,
        preferred_element_type=jnp.float32,
    )


def on_device(panel, orbitals, potential, projectors, strengths, atom_domain, patch_start):
    width_x, width_y, depth_z, columns = panel.shape
    count_node = lax.axis_size("node")
    count_orb = lax.axis_size("orb")
    previous = panel
    current = panel
    for step_index in range(DEG):
        extended = padded_2(current, (("node", 0), ("orb", 1)), 1)
        applied = operate(extended, potential)
        if step_index == 0:
            updated = applied
        else:
            updated = 2.0 * applied - previous.astype(jnp.float32)
        previous = current
        current = updated.astype(jnp.bfloat16)
    flat_panel = current.reshape(-1, columns)
    flat_orbit = orbitals.reshape(-1, orbitals.shape[3])
    grid_term = lax.dot_general(
        flat_panel, flat_orbit, (((0,), (0,)), ((), ())), preferred_element_type=jnp.float32
    )
    atom_dev = projectors.shape[0]
    capacity = max(2, (2 * atom_dev + count_node - 1) // count_node)
    domains = atom_domain[:, 0]
    matches = (domains[:, None] == jnp.arange(count_node, dtype=jnp.int32)[None, :]).astype(
        jnp.int32
    )
    before = jnp.cumsum(matches, axis=0) - matches
    position = domains * capacity + jnp.sum(before * matches, axis=1)
    value_buf = (
        jnp.zeros((count_node * capacity, projectors.shape[1]), jnp.bfloat16)
        .at[position]
        .set(projectors)
    )
    coeff_buf = jnp.zeros((count_node * capacity,), jnp.bfloat16).at[position].set(strengths)
    start_buf = jnp.zeros((count_node * capacity,), jnp.int32).at[position].set(patch_start)
    received = (
        lax.all_to_all(
            value_buf.reshape(count_node, capacity, -1),
            "node",
            split_axis=0,
            concat_axis=0,
            tiled=True,
        ),
        lax.all_to_all(
            coeff_buf.reshape(count_node, capacity), "node", split_axis=0, concat_axis=0, tiled=True
        ),
        lax.all_to_all(
            start_buf.reshape(count_node, capacity), "node", split_axis=0, concat_axis=0, tiled=True
        ),
    )
    atom_term = atom_part(
        received[0].reshape(count_node * capacity, -1),
        received[1].reshape(-1),
        received[2].reshape(-1),
        flat_panel,
        flat_orbit,
    )
    nodes_all = count_node * width_x * count_orb * width_y * depth_z
    atoms_all = atom_dev * count_node * count_orb
    partial_sum = grid_term * (1.0 / math.sqrt(nodes_all)) + atom_term * (
        1.0 / math.sqrt(atoms_all)
    )
    intersection = lax.psum(partial_sum, ("node", "orb"))
    return (current, intersection)


def solution(mesh):
    placed = (
        P("node", "orb", None, None),
        P("node", "orb", None, None),
        P("node", "orb", None),
        P(("node", "orb"), None),
        P(("node", "orb")),
        P(("node", "orb"), None),
        P(("node", "orb")),
    )
    return jax.shard_map(
        on_device,
        mesh=mesh,
        in_specs=placed,
        out_specs=(P("node", "orb", None, None), P()),
        check_vma=False,
    )
```

profile of v0, /device:TPU:1, one launch (start us, length us, event | category | flops | bytes accessed | tf_op | source)
XLA Modules:
  0.0 847.6 jit_solution(1029546064732218150)
XLA Ops:
  7.2 1.0 fusion.65
  8.2 4.6 collective-permute-start
  12.8 9.1 %collective-permute-start.1 = (bf16[1,4,128,128]{3,2,1,0:T(8,128)(2,1)S(1)}, bf16[1,4,128,128]{3,2,1,0:T(8,128)(2,1)S(1)}, u32[]{:S(2)}, u32[]{:S(2)}) collective-permute-start(bf16[1,4,128,128]{3,2,1,0:T(8,128)(2,1)S(1)} %get-tuple-element.24), channel_id=1, source_target_pairs={{16,0},{32,16},{48,32},{64,48},{80,64},{96,80},{112,96},{128,112},... | collective-permute-start | bytes 393224 | tf_op jit(solution)/shard_map/ppermute | solution.py:23
  22.0 1.0 constant_dynamic-update-slice_fusion.1
  23.1 3.7 collective-permute-start.2
  26.8 1.3 collective-permute-start.3
  28.1 0.6 collective-permute-done.2
  28.7 9.3 %collective-permute-done.3 = bf16[4,1,128,128]{3,2,1,0:T(8,128)(2,1)S(1)} collective-permute-done((bf16[4,1,128,128]{3,2,1,0:T(8,128)(2,1)S(1)}, bf16[4,1,128,128]{3,2,1,0:T(8,128)(2,1)S(1)}, u32[]{:S(2)}, u32[]{:S(2)}) %collective-permute-start.3) | collective-permute-done | bytes 131104 | tf_op jit(solution)/shard_map/ppermute | solution.py:23
  38.1 0.3 fusion.8
  38.5 7.5 collective-permute-start.4
  46.0 2.1 collective-permute-start.5
  48.1 4.9 collective-permute-done.5
  53.0 8.2 collective-permute-start.6
  61.2 1.3 collective-permute-start.7
  62.5 5.7 collective-permute-done.6
  68.2 3.3 collective-permute-done.7
  71.7 0.4 fusion.16
  72.0 6.2 collective-permute-start.8
  78.3 1.9 collective-permute-start.9
  80.2 4.3 collective-permute-done.9
  84.6 3.9 collective-permute-start.10
  88.5 1.3 collective-permute-start.11
  89.8 1.5 collective-permute-done.10
  91.4 6.1 collective-permute-done.11
  97.6 0.6 fusion.24
  98.2 4.8 collective-permute-start.12
  103.1 1.9 collective-permute-start.13
  105.3 4.0 collective-permute-done.13
  109.4 4.8 collective-permute-start.14
  114.2 1.3 collective-permute-start.15
  115.5 0.8 scatter_custom_fusion.2
  116.3 0.7 all_to_all.20
  117.1 9.7 %all-to-all-start.2 = ((bf16[48,1,2]{2,1,0:T(2,128)(2,1)}), bf16[48,1,2]{2,1,0:T(2,128)(2,1)S(1)}, u32[]{:S(2)}, u32[]{:S(2)}) async-start(bf16[48,1,2]{2,1,0:T(2,128)(2,1)} %all_to_all.20), calls=%async_computation.2 | async-start | bytes 49152 | tf_op jit(solution)/shard_map/all_to_all | solution.py:105
  126.8 0.8 scatter_custom_fusion
  127.6 0.7 all_to_all.15
  128.3 0.9 scatter_custom_fusion.1
  129.2 0.6 reshape.92
  129.8 5.7 all-to-all-done.2
  135.5 4.6 all-to-all-start
  140.3 8.5 %all-to-all-done = s32[48,1,2]{2,1,0:T(1,128)S(1)} async-done(((s32[48,1,2]{2,1,0:T(1,128)}), s32[48,1,2]{2,1,0:T(1,128)S(1)}, u32[]{:S(2)}, u32[]{:S(2)}) %all-to-all-start) | async-done | bytes 416 | tf_op jit(solution)/shard_map/all_to_all | solution.py:108
  148.8 4.7 all-to-all-start.1
  153.6 0.5 broadcast.158
  154.1 0.7 reduce.11
  155.1 0.4 fusion.32
  155.5 3.5 collective-permute-start.16
  159.1 1.9 collective-permute-start.17
  161.1 4.3 collective-permute-done.17
  165.4 8.4 collective-permute-start.18
  173.8 1.3 collective-permute-start.19
  175.3 0.4 collective-permute-done.18
  175.7 6.6 collective-permute-done.19
  182.4 0.4 fusion.40
  182.8 3.6 collective-permute-start.20
  186.5 2.1 collective-permute-start.21
  188.7 168.5 %scatter_custom_fusion.3 = bf16[98304]{0:T(1024)(128)(2,1)S(1)} fusion(s32[24576]{0:T(1024)S(1)} %bitcast.32, bf16[24576]{0:T(1024)(128)(2,1)S(1)} %bitcast.33, bf16[]{:T(256)} %constant.42.clone.1), kind=kCustom, calls=%fused_computation.111 | custom fusion | bytes 196610
  357.3 12.8 %collective-permute-start.22 = (bf16[4,1,128,128]{3,2,1,0:T(8,128)(2,1)S(1)}, bf16[4,1,128,128]{3,2,1,0:T(8,128)(2,1)S(1)}, u32[]{:S(2)}, u32[]{:S(2)}) collective-permute-start(bf16[4,1,128,128]{3,2,1,0:T(8,128)(2,1)S(1)} %get-tuple-element.2), channel_id=1, source_target_pairs={{0,1},{1,2},{2,3},{3,4},{4,5},{5,6},{6,7},{7,8},{8,9},{9,10},{10,1... | collective-permute-start | bytes 393224 | tf_op jit(solution)/shard_map/ppermute | solution.py:20
  370.1 1.3 collective-permute-start.23
  371.7 0.4 collective-permute-done.22
  372.0 5.6 collective-permute-done.23
  377.8 0.4 fusion.48
  378.2 0.3 fusion.1
  378.7 1.0 fusion
  379.6 459.6 %all-reduce.8.cloned.1.call-done = f32[128,256]{1,0:T(8,128)} async-done(((f32[128,256]{1,0:T(8,128)}), f32[128,256]{1,0:T(8,128)}) %all-reduce.8.cloned.1.call-update) | async-done | bytes 131088 | tf_op jit(solution)/shard_map/psum | solution.py:124
  839.2 1.6 copy.21
  (64 shorter events, 2.8 us)
Async XLA Ops:
  7.2 364.3 %copy-start = (bf16[2,4,128,256]{3,2,1,0:T(8,128)(2,1)S(1)}, bf16[2,4,128,256]{3,2,1,0:T(8,128)(2,1)}, u32[]{:S(2)}) copy-start(bf16[2,4,128,256]{3,2,1,0:T(8,128)(2,1)} %param.8) | copy-start | bytes 1572868
  7.2 20.9 %copy-start.3 = (f32[2,4,128]{2,1,0:T(4,128)S(1)}, f32[2,4,128]{2,1,0:T(4,128)}, u32[]{:S(2)}) copy-start(f32[2,4,128]{2,1,0:T(4,128)} %param.9) | copy-start | bytes 12292
  8.2 13.7 %collective-permute-start = (bf16[1,4,128,128]{3,2,1,0:T(8,128)(2,1)S(1)}, bf16[1,4,128,128]{3,2,1,0:T(8,128)(2,1)S(1)}, u32[]{:S(2)}, u32[]{:S(2)}) collective-permute-start(bf16[1,4,128,128]{3,2,1,0:T(8,128)(2,1)S(1)} %get-tuple-element.25), channel_id=1, source_target_pairs={{0,16},{16,32},{32,48},{48,64},{64,80},{80,96},{96,112},{112,128},... | collective-permute-start | bytes 393224 | tf_op jit(solution)/shard_map/ppermute | solution.py:20
  12.8 10.2 %collective-permute-start.1 = (bf16[1,4,128,128]{3,2,1,0:T(8,128)(2,1)S(1)}, bf16[1,4,128,128]{3,2,1,0:T(8,128)(2,1)S(1)}, u32[]{:S(2)}, u32[]{:S(2)}) collective-permute-start(bf16[1,4,128,128]{3,2,1,0:T(8,128)(2,1)S(1)} %get-tuple-element.24), channel_id=1, source_target_pairs={{16,0},{32,16},{48,32},{64,48},{80,64},{96,80},{112,96},{128,112},... | collective-permute-start | bytes 393224 | tf_op jit(solution)/shard_map/ppermute | solution.py:23
  23.1 5.7 collective-permute-start.2
  26.8 11.2 %collective-permute-start.3 = (bf16[4,1,128,128]{3,2,1,0:T(8,128)(2,1)S(1)}, bf16[4,1,128,128]{3,2,1,0:T(8,128)(2,1)S(1)}, u32[]{:S(2)}, u32[]{:S(2)}) collective-permute-start(bf16[4,1,128,128]{3,2,1,0:T(8,128)(2,1)S(1)} %get-tuple-element.13), channel_id=1, source_target_pairs={{1,0},{2,1},{3,2},{4,3},{5,4},{6,5},{7,6},{8,7},{9,8},{10,9},{11,1... | collective-permute-start | bytes 393224 | tf_op jit(solution)/shard_map/ppermute | solution.py:23
  38.5 9.6 %collective-permute-start.4 = (bf16[1,4,128,128]{3,2,1,0:T(8,128)(2,1)S(1)}, bf16[1,4,128,128]{3,2,1,0:T(8,128)(2,1)S(1)}, u32[]{:S(2)}, u32[]{:S(2)}) collective-permute-start(bf16[1,4,128,128]{3,2,1,0:T(8,128)(2,1)S(1)} %get-tuple-element.22), channel_id=1, source_target_pairs={{0,16},{16,32},{32,48},{48,64},{64,80},{80,96},{96,112},{112,128},... | collective-permute-start | bytes 393224 | tf_op jit(solution)/shard_map/ppermute | solution.py:20
  46.0 25.7 %copy-start.2 = (bf16[2,4,128,128]{3,2,1,0:T(8,128)(2,1)S(1)}, bf16[2,4,128,128]{3,2,1,0:T(8,128)(2,1)}, u32[]{:S(2)}) copy-start(bf16[2,4,128,128]{3,2,1,0:T(8,128)(2,1)} %param.7) | copy-start | bytes 786436
  46.0 6.9 collective-permute-start.5
  53.0 15.2 %collective-permute-start.6 = (bf16[4,1,128,128]{3,2,1,0:T(8,128)(2,1)S(1)}, bf16[4,1,128,128]{3,2,1,0:T(8,128)(2,1)S(1)}, u32[]{:S(2)}, u32[]{:S(2)}) collective-permute-start(bf16[4,1,128,128]{3,2,1,0:T(8,128)(2,1)S(1)} %get-tuple-element.10), channel_id=1, source_target_pairs={{0,1},{1,2},{2,3},{3,4},{4,5},{5,6},{6,7},{7,8},{8,9},{9,10},{10,1... | collective-permute-start | bytes 393224 | tf_op jit(solution)/shard_map/ppermute | solution.py:20
  61.2 10.3 %collective-permute-start.7 = (bf16[4,1,128,128]{3,2,1,0:T(8,128)(2,1)S(1)}, bf16[4,1,128,128]{3,2,1,0:T(8,128)(2,1)S(1)}, u32[]{:S(2)}, u32[]{:S(2)}) collective-permute-start(bf16[4,1,128,128]{3,2,1,0:T(8,128)(2,1)S(1)} %get-tuple-element.11), channel_id=1, source_target_pairs={{1,0},{2,1},{3,2},{4,3},{5,4},{6,5},{7,6},{8,7},{9,8},{10,9},{11,1... | collective-permute-start | bytes 393224 | tf_op jit(solution)/shard_map/ppermute | solution.py:23
  72.0 8.2 collective-permute-start.8
  78.3 6.3 collective-permute-start.9
  84.6 6.8 collective-permute-start.10
  88.5 8.9 %collective-permute-start.11 = (bf16[4,1,128,128]{3,2,1,0:T(8,128)(2,1)S(1)}, bf16[4,1,128,128]{3,2,1,0:T(8,128)(2,1)S(1)}, u32[]{:S(2)}, u32[]{:S(2)}) collective-permute-start(bf16[4,1,128,128]{3,2,1,0:T(8,128)(2,1)S(1)} %get-tuple-element.9), channel_id=1, source_target_pairs={{1,0},{2,1},{3,2},{4,3},{5,4},{6,5},{7,6},{8,7},{9,8},{10,9},{11,1... | collective-permute-start | bytes 393224 | tf_op jit(solution)/shard_map/ppermute | solution.py:23
  97.6 7.4 copy-start.4
  98.2 7.1 collective-permute-start.12
  103.1 6.3 collective-permute-start.13
  109.4 45.6 %collective-permute-start.14 = (bf16[4,1,128,128]{3,2,1,0:T(8,128)(2,1)S(1)}, bf16[4,1,128,128]{3,2,1,0:T(8,128)(2,1)S(1)}, u32[]{:S(2)}, u32[]{:S(2)}) collective-permute-start(bf16[4,1,128,128]{3,2,1,0:T(8,128)(2,1)S(1)} %get-tuple-element.6), channel_id=1, source_target_pairs={{0,1},{1,2},{2,3},{3,4},{4,5},{5,6},{6,7},{7,8},{8,9},{9,10},{10,1... | collective-permute-start | bytes 393224 | tf_op jit(solution)/shard_map/ppermute | solution.py:20
  114.2 40.8 %collective-permute-start.15 = (bf16[4,1,128,128]{3,2,1,0:T(8,128)(2,1)S(1)}, bf16[4,1,128,128]{3,2,1,0:T(8,128)(2,1)S(1)}, u32[]{:S(2)}, u32[]{:S(2)}) collective-permute-start(bf16[4,1,128,128]{3,2,1,0:T(8,128)(2,1)S(1)} %get-tuple-element.7), channel_id=1, source_target_pairs={{1,0},{2,1},{3,2},{4,3},{5,4},{6,5},{7,6},{8,7},{9,8},{10,9},{11,1... | collective-permute-start | bytes 393224 | tf_op jit(solution)/shard_map/ppermute | solution.py:23
  117.1 18.4 %all-to-all-start.2 = ((bf16[48,1,2]{2,1,0:T(2,128)(2,1)}), bf16[48,1,2]{2,1,0:T(2,128)(2,1)S(1)}, u32[]{:S(2)}, u32[]{:S(2)}) async-start(bf16[48,1,2]{2,1,0:T(2,128)(2,1)} %all_to_all.20), calls=%async_computation.2 | async-start | bytes 49152 | tf_op jit(solution)/shard_map/all_to_all | solution.py:105
  135.5 13.3 %all-to-all-start = ((s32[48,1,2]{2,1,0:T(1,128)}), s32[48,1,2]{2,1,0:T(1,128)S(1)}, u32[]{:S(2)}, u32[]{:S(2)}) async-start(s32[48,1,2]{2,1,0:T(1,128)} %bitcast.5), calls=%async_computation | async-start | bytes 49152 | tf_op jit(solution)/shard_map/all_to_all | solution.py:108
  148.8 39.8 %all-to-all-start.1 = ((bf16[48,2,256]{2,1,0:T(2,128)(2,1)}), bf16[48,2,256]{2,1,0:T(2,128)(2,1)S(1)}, u32[]{:S(2)}, u32[]{:S(2)}) async-start(bf16[48,2,256]{2,1,0:T(2,128)(2,1)} %reshape.92), calls=%async_computation.1 | async-start | bytes 98304 | tf_op jit(solution)/shard_map/all_to_all | solution.py:98
  153.5 685.7 %all-reduce.8.cloned.1.call-start = ((), (), s32[]{:S(2)}) async-start(), calls=%async_computation.3 | async-start | bytes 262144 | tf_op jit(solution)/shard_map/psum | solution.py:124
  155.1 20.0 %copy-start.6 = (s32[2]{0:T(128)S(1)}, s32[2]{0:T(128)}, u32[]{:S(2)}) copy-start(s32[2]{0:T(128)} %constant.67) | copy-start | bytes 28
  155.5 19.7 %copy-start.5 = (s32[2]{0:T(128)S(1)}, s32[2]{0:T(128)}, u32[]{:S(2)}) copy-start(s32[2]{0:T(128)} %constant.70) | copy-start | bytes 28
  155.5 5.6 collective-permute-start.16
  159.1 6.3 collective-permute-start.17
  165.4 10.3 %collective-permute-start.18 = (bf16[4,1,128,128]{3,2,1,0:T(8,128)(2,1)S(1)}, bf16[4,1,128,128]{3,2,1,0:T(8,128)(2,1)S(1)}, u32[]{:S(2)}, u32[]{:S(2)}) collective-permute-start(bf16[4,1,128,128]{3,2,1,0:T(8,128)(2,1)S(1)} %get-tuple-element.4), channel_id=1, source_target_pairs={{0,1},{1,2},{2,3},{3,4},{4,5},{5,6},{6,7},{7,8},{8,9},{9,10},{10,1... | collective-permute-start | bytes 393224 | tf_op jit(solution)/shard_map/ppermute | solution.py:20
  173.8 8.5 %collective-permute-start.19 = (bf16[4,1,128,128]{3,2,1,0:T(8,128)(2,1)S(1)}, bf16[4,1,128,128]{3,2,1,0:T(8,128)(2,1)S(1)}, u32[]{:S(2)}, u32[]{:S(2)}) collective-permute-start(bf16[4,1,128,128]{3,2,1,0:T(8,128)(2,1)S(1)} %get-tuple-element.5), channel_id=1, source_target_pairs={{1,0},{2,1},{3,2},{4,3},{5,4},{6,5},{7,6},{8,7},{9,8},{10,9},{11,1... | collective-permute-start | bytes 393224 | tf_op jit(solution)/shard_map/ppermute | solution.py:23
  182.8 174.4 %collective-permute-start.20 = (bf16[1,4,128,128]{3,2,1,0:T(8,128)(2,1)S(1)}, bf16[1,4,128,128]{3,2,1,0:T(8,128)(2,1)S(1)}, u32[]{:S(2)}, u32[]{:S(2)}) collective-permute-start(bf16[1,4,128,128]{3,2,1,0:T(8,128)(2,1)S(1)} %get-tuple-element.14), channel_id=1, source_target_pairs={{0,16},{16,32},{32,48},{48,64},{64,80},{80,96},{96,112},{112,128},... | collective-permute-start | bytes 393224 | tf_op jit(solution)/shard_map/ppermute | solution.py:20
  186.5 170.8 %collective-permute-start.21 = (bf16[1,4,128,128]{3,2,1,0:T(8,128)(2,1)S(1)}, bf16[1,4,128,128]{3,2,1,0:T(8,128)(2,1)S(1)}, u32[]{:S(2)}, u32[]{:S(2)}) collective-permute-start(bf16[1,4,128,128]{3,2,1,0:T(8,128)(2,1)S(1)} %get-tuple-element.15), channel_id=1, source_target_pairs={{16,0},{32,16},{48,32},{64,48},{80,64},{96,80},{112,96},{128,112},... | collective-permute-start | bytes 393224 | tf_op jit(solution)/shard_map/ppermute | solution.py:23
  357.3 14.7 %collective-permute-start.22 = (bf16[4,1,128,128]{3,2,1,0:T(8,128)(2,1)S(1)}, bf16[4,1,128,128]{3,2,1,0:T(8,128)(2,1)S(1)}, u32[]{:S(2)}, u32[]{:S(2)}) collective-permute-start(bf16[4,1,128,128]{3,2,1,0:T(8,128)(2,1)S(1)} %get-tuple-element.2), channel_id=1, source_target_pairs={{0,1},{1,2},{2,3},{3,4},{4,5},{5,6},{6,7},{7,8},{8,9},{9,10},{10,1... | collective-permute-start | bytes 393224 | tf_op jit(solution)/shard_map/ppermute | solution.py:20
  370.1 7.5 collective-permute-start.23
  378.2 462.7 %copy-start.1 = (bf16[2,4,128,128]{3,2,1,0:T(8,128)(2,1)}, bf16[2,4,128,128]{3,2,1,0:T(8,128)(2,1)S(1)}, u32[]{:S(2)}) copy-start(bf16[2,4,128,128]{3,2,1,0:T(8,128)(2,1)S(1)} %fusion.48) | copy-start | bytes 786436
Sparse Core Ops, SparseCore 0:
  379.8 459.4 all-reduce.7
where the time goes:
time: 849 us; the launch traced here: 848 us
  waiting for transfers between devices  531 us (63%)
  local copies, waits for them, and re-layouts  178 us (21%)
  starting transfers between devices  118 us (14%)
  between operations  14.7 us (2%)
    psum x1, waiting for transfers between devices, on_device(): intersection = lax.psum(partial_sum, ('node', 'orb'))  460 us
    unnamed x20, local copies, waits for them, and re-layouts  171 us
    ppermute x12, starting transfers between devices, padded_2(): lax.ppermute(lax.slice_in_dim(block, block.shape[dim] - width, None, axis...  72.1 us
    ppermute x12, waiting for transfers between devices, padded_2(): lax.ppermute(lax.slice_in_dim(block, 0, width, axis=dim), axis, backward)  48.3 us
    ppermute x12, starting transfers between devices, padded_2(): lax.ppermute(lax.slice_in_dim(block, 0, width, axis=dim), axis, backward)  26.8 us
  transfers between devices with their start and end apart: 28, of which 17 were waited for; matrix products, arithmetic and copies ran while one was open for 21% of the time, Pallas kernels for 0%

commit v1 on v0

v1 whole, which is shorter than its diff:
```python
import functools
import math

import jax
import jax.numpy as jnp
from jax import lax
from jax.experimental import pallas as pl
from jax.experimental.pallas import tpu as pltpu
from jax.sharding import PartitionSpec as P

DEG = 6
CHUNKS = 4
MESH = pl.DeviceIdType.MESH
SHIFT_POINT = 5.25
HALF_RANGE = 3.25


def factors(count_node, count_orb):
    if (count_node, count_orb) == (48, 16):
        return 3, 8, 4, 4
    ny = max(1, min(count_node // 2, 8))
    return count_node // (2 * ny), ny, max(1, count_orb // 4), min(count_orb, 4)


def kernel(
    dims,
    scales,
    panel_ref,
    orbit_ref,
    pot_ref,
    proj_ref,
    str_ref,
    dom_ref,
    start_ref,
    out_ref,
    inter_ref,
    y,
    hxl,
    hxh,
    hyl,
    hyh,
    diag,
    orb_v,
    w_ref,
    m_ref,
    apack,
    abuf,
    part,
    rs,
    ar_src,
    ar,
    ag_src,
    ag,
    load_sem,
    out_sem,
    hsend,
    hrecv,
    asend,
    arecv,
    rsend,
    rrecv,
):
    n_node, n_orb, nzl, ny, nx, nzh = dims
    c1, ratio = scales
    node = lax.axis_index("node")
    orb = lax.axis_index("orb")
    core = lax.rem(node, 2)
    yy = lax.rem(node // 2, ny)
    zl = node // (2 * ny)
    xx = orb // nzh
    zh = lax.rem(orb, nzh)
    n_xy = nx * ny
    n_zc = nzh * nzl * 2
    wx, wy, nz, cols = panel_ref.shape
    ch = nz // CHUNKS

    load_panel = pltpu.make_async_copy(panel_ref, y.at[0], load_sem.at[0])
    load_panel.start()
    load_orbit = pltpu.make_async_copy(orbit_ref, orb_v, load_sem.at[1])
    load_orbit.start()

    barrier = pltpu.get_barrier_semaphore()

    def greet(target_node, target_orb):
        pl.semaphore_signal(
            barrier, inc=1, device_id=(target_node, target_orb), device_id_type=MESH
        )

    def greet_node(i, carry):
        greet(lax.rem(node + i, n_node), orb)
        return carry

    lax.fori_loop(1, n_node, greet_node, 0)

    def greet_x(i, carry):
        gx = lax.rem(xx + 1 + i // ny, nx)
        gy = lax.rem(i, ny)
        greet((zl * ny + gy) * 2 + core, gx * nzh + zh)
        return carry

    lax.fori_loop(0, (nx - 1) * ny, greet_x, 0)

    def greet_z(i, carry):
        gz = lax.rem(zh + 1 + i // (2 * nzl), nzh)
        rest = lax.rem(i, 2 * nzl)
        greet(((rest // 2) * ny + yy) * 2 + lax.rem(rest, 2), xx * nzh + gz)
        return carry

    lax.fori_loop(0, (nzh - 1) * 2 * nzl, greet_z, 0)
    greeted = (n_node - 1) + (nx - 1) * ny + (nzh - 1) * 2 * nzl
    up_cross = jnp.logical_and(zh == nzh - 1, orb < n_orb - 1)
    down_cross = jnp.logical_and(zh == 0, orb > 0)

    @pl.when(up_cross)
    def _():
        greet(node, orb + 1)

    @pl.when(down_cross)
    def _():
        greet(node, orb - 1)

    crossings = up_cross.astype(jnp.int32) + down_cross.astype(jnp.int32)
    pl.semaphore_wait(barrier, greeted + crossings)

    def halo(side, k, c):
        zs = pl.ds(c * ch, ch)
        if side == 0:
            src, dst, target = y.at[k, wx - 1, :, zs], hxl.at[k, :, zs], (node + 1, orb)
        elif side == 1:
            src, dst, target = y.at[k, 0, :, zs], hxh.at[k, :, zs], (node - 1, orb)
        elif side == 2:
            src, dst, target = y.at[k, :, wy - 1, zs], hyl.at[k, :, zs], (node, orb + 1)
        else:
            src, dst, target = y.at[k, :, 0, zs], hyh.at[k, :, zs], (node, orb - 1)
        return pltpu.make_async_remote_copy(
            src_ref=src,
            dst_ref=dst,
            send_sem=hsend.at[side],
            recv_sem=hrecv.at[k, side, c],
            device_id=target,
            device_id_type=MESH,
        )

    sends = (node < n_node - 1, node > 0, orb < n_orb - 1, orb > 0)
    receives = (node > 0, node < n_node - 1, orb > 0, orb < n_orb - 1)

    def send_halo(k, c):
        for side in (2, 3, 0, 1):

            @pl.when(sends[side])
            def _(side=side):
                halo(side, k, c).start()

    def wait_halo(k, c):
        for side in (0, 1, 2, 3):

            @pl.when(receives[side])
            def _(side=side):
                halo(side, k, c).wait_recv()

    load_panel.wait()
    for c in range(CHUNKS):
        send_halo(0, c)

    for side, buf in enumerate((hxl, hxh, hyl, hyh)):

        @pl.when(jnp.logical_not(receives[side]))
        def _(buf=buf):
            def clear(k, carry):
                buf[k] = jnp.zeros(buf.shape[1:], buf.dtype)
                return carry

            lax.fori_loop(0, DEG, clear, 0)

    atoms = proj_ref.shape[0]
    f32 = jnp.float32
    a_sub = lax.broadcasted_iota(jnp.int32, (atoms, atoms), 0)
    a_lane = lax.broadcasted_iota(jnp.int32, (atoms, atoms), 1)
    eye = a_sub == a_lane

    def column(row):
        return jnp.sum(jnp.where(eye, jnp.broadcast_to(row, (atoms, atoms)), 0), axis=1, keepdims=True)

    dom_row = dom_ref[...]
    start_row = start_ref[...]
    dom_col = column(dom_row)
    start_col = column(start_row)
    str_col = column(str_ref[...].astype(f32))
    hi_col = start_col // 128
    lo_col = start_col - hi_col * 128
    same = jnp.logical_and(jnp.broadcast_to(dom_col, (atoms, atoms)) == dom_row, a_sub < a_lane)
    rank_row = jnp.sum(jnp.where(same, 1, 0), axis=0, keepdims=True)
    halves = []
    for half in range(2):
        piece = proj_ref[:, half * 128 : (half + 1) * 128].astype(f32)
        for bit in range(7):
            taken = ((lo_col // (1 << bit)) - 2 * (lo_col // (2 << bit))) == 1
            piece = jnp.where(taken, pltpu.roll(piece, 1 << bit, 1), piece)
        halves.append(piece)
    lane = lax.broadcasted_iota(jnp.int32, (atoms, 128), 1)
    meta = jnp.where(
        lane == 0,
        lo_col.astype(f32),
        jnp.where(lane == 1, hi_col.astype(f32), jnp.where(lane == 2, str_col, 0.0)),
    )
    rows = lax.broadcasted_iota(jnp.int32, (n_node * 8, atoms), 0)
    slot_dom = rows // 8
    slot_row = rows - slot_dom * 8
    named = slot_dom == dom_row
    packed = None
    for code, piece in ((2 * rank_row, halves[0]), (2 * rank_row + 1, halves[1]), (4 + rank_row, meta)):
        choose = jnp.where(jnp.logical_and(named, slot_row == code), 1.0, 0.0)
        term = jnp.dot(choose, piece, preferred_element_type=f32)
        packed = term if packed is None else packed + term
    apack[...] = packed.reshape(n_node, 8, 128)

    def atom_copy(i):
        other = lax.rem(node + i, n_node)
        return pltpu.make_async_remote_copy(
            src_ref=apack.at[other],
            dst_ref=abuf.at[node],
            send_sem=asend,
            recv_sem=arecv,
            device_id=(other, orb),
            device_id_type=MESH,
        )

    def send_atoms(i, carry):
        atom_copy(i).start()
        return carry

    lax.fori_loop(1, n_node, send_atoms, 0)
    abuf[node] = apack[node]

    for ix in range(wx):
        for iy in range(wy):
            row = pot_ref[ix * wy + iy : ix * wy + iy + 1, :]
            diag[ix, iy] = (jnp.broadcast_to(row, (nz, nz)).T - (SHIFT_POINT - 3.0)) * (1.0 / HALF_RANGE)

    z_out = lax.broadcasted_iota(jnp.int32, (nz, nz), 0)
    z_in = lax.broadcasted_iota(jnp.int32, (nz, nz), 1)
    beside = jnp.where(jnp.abs(z_out - z_in) == 1, 1.0, 0.0).astype(jnp.bfloat16)

    def step(k, carry):
        twice = jnp.where(k == 0, 1.0, 2.0).astype(f32)
        less = jnp.where(k == 0, 0.0, 1.0).astype(f32)
        before = lax.max(k - 1, 0)
        arm = twice * (0.5 / HALF_RANGE)
        for c in range(CHUNKS):
            zs = pl.ds(c * ch, ch)
            here = [[y[k, ix, iy, zs].astype(f32) for iy in range(wy)] for ix in range(wx)]
            base = []
            for ix in range(wx):
                line = []
                for iy in range(wy):
                    total = jnp.dot(
                        beside[c * ch : (c + 1) * ch], y[k, ix, iy], preferred_element_type=f32
                    )
                    total = total + here[1 - ix][iy]
                    if iy > 0:
                        total = total + here[ix][iy - 1]
                    if iy < wy - 1:
                        total = total + here[ix][iy + 1]
                    old = y[before, ix, iy, zs].astype(f32)
                    line.append(
                        (twice * diag[ix, iy, zs]) * here[ix][iy] - arm * total - less * old
                    )
                base.append(line)
            wait_halo(k, c)
            for ix in range(wx):
                for iy in range(wy):
                    side = (hxl if ix == 0 else hxh)[k, iy, zs].astype(f32)
                    if iy == 0:
                        side = side + hyl[k, ix, zs].astype(f32)
                    if iy == wy - 1:
                        side = side + hyh[k, ix, zs].astype(f32)
                    y[k + 1, ix, iy, zs] = (base[ix][iy] - arm * side).astype(jnp.bfloat16)

            @pl.when(k < DEG - 1)
            def _():
                send_halo(lax.min(k + 1, DEG - 1), c)

        return carry

    lax.fori_loop(0, DEG // 2, step, 0)

    pltpu.make_async_remote_copy(
        src_ref=abuf.at[pl.ds(0, n_node - 1)],
        dst_ref=abuf.at[pl.ds(0, n_node - 1)],
        send_sem=asend,
        recv_sem=arecv,
        device_id=(lax.rem(node + 1, n_node), orb),
        device_id_type=MESH,
    ).wait_recv()
    load_orbit.wait()
    blocks = wx * wy
    s_lane = lax.broadcasted_iota(jnp.int32, (n_node, 128), 1).astype(f32)
    coeffs = []
    for slot in range(2):
        v0 = abuf[:, 2 * slot, :]
        v1 = abuf[:, 2 * slot + 1, :]
        info = abuf[:, 4 + slot, :]
        lo, hi, coeff = info[:, 0:1], info[:, 1:2], info[:, 2:3]
        inside = s_lane >= lo
        placed = (
            jnp.where(inside, v0, 0.0),
            jnp.where(inside, v1, v0),
            jnp.where(inside, 0.0, v1),
        )
        for j in range(blocks):
            total = jnp.zeros((n_node, 128), f32)
            for ahead in range(3):
                if j >= ahead:
                    total = total + jnp.where(hi == float(j - ahead), placed[ahead], 0.0)
            w_ref[slot * n_node : (slot + 1) * n_node, j * 128 : (j + 1) * 128] = total.astype(
                jnp.bfloat16
            )
        coeffs.append(coeff)
    flat_orbit = orb_v[...].reshape(blocks * nz, -1)
    norb = flat_orbit.shape[1]
    proj = jnp.dot(w_ref[...], flat_orbit, preferred_element_type=f32)
    proj = proj * (jnp.concatenate(coeffs, axis=0) * ratio)
    proj_hi = proj.astype(jnp.bfloat16)
    proj_lo = (proj - proj_hi.astype(f32)).astype(jnp.bfloat16)
    proj_both = jnp.concatenate([proj_hi, proj_lo], axis=1)
    for j in range(blocks):
        both = lax.dot_general(
            w_ref[:, j * 128 : (j + 1) * 128],
            proj_both,
            (((0,), (0,)), ((), ())),
            preferred_element_type=f32,
        )
        whole = both[:, :norb] + both[:, norb:] + orb_v[j // wy, j % wy].astype(f32)
        whole_hi = whole.astype(jnp.bfloat16)
        m_ref[j * 128 : (j + 1) * 128, :norb] = whole_hi
        m_ref[j * 128 : (j + 1) * 128, norb:] = (whole - whole_hi.astype(f32)).astype(jnp.bfloat16)

    lax.fori_loop(DEG // 2, DEG, step, 0)

    save = pltpu.make_async_copy(y.at[DEG], out_ref, out_sem)
    save.start()
    both = lax.dot_general(
        y[DEG].reshape(blocks * nz, cols),
        m_ref[...],
        (((0,), (0,)), ((), ())),
        preferred_element_type=f32,
    )
    share = (both[:, :norb] + both[:, norb:]) * c1
    wide = norb // 128
    tiles = (cols // 8) * wide
    per = tiles // n_xy
    for t in range(tiles):
        part[t // per, (t % per) * 8 : (t % per + 1) * 8, :] = share[
            (t // wide) * 8 : (t // wide + 1) * 8, (t % wide) * 128 : (t % wide + 1) * 128
        ]

    me_xy = xx * ny + yy
    me_zc = (zh * nzl + zl) * 2 + core

    def plane_target(i):
        g = lax.rem(me_xy + i, n_xy)
        gy = lax.rem(g, ny)
        return g, ((zl * ny + gy) * 2 + core, (g // ny) * nzh + zh)

    def line_target(i):
        g = lax.rem(me_zc + i, n_zc)
        gz = g // 2
        return g, ((lax.rem(gz, nzl) * ny + yy) * 2 + lax.rem(g, 2), xx * nzh + gz // nzl)

    def exchange(stage, count, target_of, source_of, dst, mine):
        def send(i, carry):
            g, target = target_of(i)
            pltpu.make_async_remote_copy(
                src_ref=source_of(g),
                dst_ref=dst.at[mine],
                send_sem=rsend.at[stage],
                recv_sem=rrecv.at[stage],
                device_id=target,
                device_id_type=MESH,
            ).start()
            return carry

        lax.fori_loop(1, count, send, 0)

    def arrived(stage, count, target_of, dst):
        pltpu.make_async_remote_copy(
            src_ref=dst.at[pl.ds(0, count - 1)],
            dst_ref=dst.at[pl.ds(0, count - 1)],
            send_sem=rsend.at[stage],
            recv_sem=rrecv.at[stage],
            device_id=target_of(1)[1],
            device_id_type=MESH,
        ).wait()

    exchange(0, n_xy, plane_target, lambda g: part.at[g], rs, me_xy)
    rs[me_xy] = part[me_xy]
    arrived(0, n_xy, plane_target, rs)
    own = jnp.sum(rs[...], axis=0)
    ar_src[...] = own
    exchange(1, n_zc, line_target, lambda g: ar_src, ar, me_zc)
    ar[me_zc] = own
    arrived(1, n_zc, line_target, ar)
    own = jnp.sum(ar[...], axis=0)
    ag_src[...] = own
    exchange(2, n_xy, plane_target, lambda g: ag_src, ag, me_xy)
    ag[me_xy] = own
    arrived(2, n_xy, plane_target, ag)
    for t in range(tiles):
        inter_ref[
            (t // wide) * 8 : (t // wide + 1) * 8, (t % wide) * 128 : (t % wide + 1) * 128
        ] = ag[t // per, (t % per) * 8 : (t % per + 1) * 8, :]

    for side, buf in enumerate((hxl, hxh, hyl, hyh)):

        @pl.when(sends[side])
        def _(side=side, buf=buf):
            pltpu.make_async_remote_copy(
                src_ref=buf,
                dst_ref=buf,
                send_sem=hsend.at[side],
                recv_sem=hrecv.at[0, side, 0],
                device_id=(lax.rem(node + 1, n_node), orb),
                device_id_type=MESH,
            ).wait_send()

    pltpu.make_async_remote_copy(
        src_ref=abuf.at[pl.ds(0, n_node - 1)],
        dst_ref=abuf.at[pl.ds(0, n_node - 1)],
        send_sem=asend,
        recv_sem=arecv,
        device_id=(lax.rem(node + 1, n_node), orb),
        device_id_type=MESH,
    ).wait_send()
    save.wait()


def on_device(panel, orbitals, potential, projectors, strengths, atom_domain, patch_start):
    wx, wy, nz, cols = panel.shape
    norb = orbitals.shape[3]
    n_node = lax.axis_size("node")
    n_orb = lax.axis_size("orb")
    nzl, ny, nx, nzh = factors(n_node, n_orb)
    n_xy, n_zc = nx * ny, nzh * nzl * 2
    atoms = projectors.shape[0]
    nodes_all = n_node * wx * n_orb * wy * nz
    atoms_all = atoms * n_node * n_orb
    c1 = 1.0 / math.sqrt(nodes_all)
    ratio = math.sqrt(nodes_all) / math.sqrt(atoms_all)
    rows = (cols // 8) * (norb // 128) // n_xy * 8
    bf16, f32 = jnp.bfloat16, jnp.float32
    vmem = pl.BlockSpec(memory_space=pltpu.VMEM)
    hbm = pl.BlockSpec(memory_space=pl.ANY)
    dma = pltpu.SemaphoreType.DMA
    return pl.pallas_call(
        functools.partial(kernel, (n_node, n_orb, nzl, ny, nx, nzh), (c1, ratio)),
        out_shape=(
            jax.ShapeDtypeStruct(panel.shape, bf16),
            jax.ShapeDtypeStruct((cols, norb), f32),
        ),
        in_specs=[hbm, hbm] + [vmem] * 5,
        out_specs=(hbm, vmem),
        scratch_shapes=[
            pltpu.VMEM((DEG + 1, wx, wy, nz, cols), bf16),
            pltpu.VMEM((DEG, wy, nz, cols), bf16),
            pltpu.VMEM((DEG, wy, nz, cols), bf16),
            pltpu.VMEM((DEG, wx, nz, cols), bf16),
            pltpu.VMEM((DEG, wx, nz, cols), bf16),
            pltpu.VMEM((wx, wy, nz, cols), f32),
            pltpu.VMEM((wx, wy, nz, norb), bf16),
            pltpu.VMEM((2 * n_node, wx * wy * nz), bf16),
            pltpu.VMEM((wx * wy * nz, 2 * norb), bf16),
            pltpu.VMEM((n_node, 8, 128), f32),
            pltpu.VMEM((n_node, 8, 128), f32),
            pltpu.VMEM((n_xy, rows, 128), f32),
            pltpu.VMEM((n_xy, rows, 128), f32),
            pltpu.VMEM((rows, 128), f32),
            pltpu.VMEM((n_zc, rows, 128), f32),
            pltpu.VMEM((rows, 128), f32),
            pltpu.VMEM((n_xy, rows, 128), f32),
            dma((2,)),
            dma,
            dma((4,)),
            dma((DEG, 4, CHUNKS)),
            dma,
            dma,
            dma((3,)),
            dma((3,)),
        ],
        compiler_params=pltpu.CompilerParams(
            collective_id=0, has_side_effects=True, vmem_limit_bytes=48 * 1024 * 1024
        ),
    )(
        panel,
        orbitals,
        potential.reshape(wx * wy, nz),
        projectors,
        strengths.reshape(1, atoms),
        atom_domain.reshape(1, atoms),
        patch_start.reshape(1, atoms),
    )


def solution(mesh):
    placed = (
        P("node", "orb", None, None),
        P("node", "orb", None, None),
        P("node", "orb", None),
        P(("node", "orb"), None),
        P(("node", "orb")),
        P(("node", "orb"), None),
        P(("node", "orb")),
    )
    return jax.shard_map(
        on_device,
        mesh=mesh,
        in_specs=placed,
        out_specs=(P("node", "orb", None, None), P()),
        check_vma=False,
    )
```

time: 849 us -> 88.1 us (0.10)
  waiting for transfers between devices: 531 us -> 0 us
  local copies, waits for them, and re-layouts: 178 us -> 4.73 us
  starting transfers between devices: 118 us -> 0 us
  Pallas kernels: 0 us -> 82.4 us
  between operations: 14.7 us -> 0.68 us
    psum x1 -> x0, waiting for transfers between devices: 460 us -> none  [on_device(): intersection = lax.psum(partial_sum, ('node', 'orb'))]
    unnamed x20 -> x16, local copies, waits for them, and re-layouts: 171 us -> 4.73 us
    ppermute x24 -> x0, starting transfers between devices: 98.9 us -> none  [the longest x12 72.1 us: padded_2(): lax.ppermute(lax.slice_in_dim(block, block.shape[dim] - width, None, axis...]
    pallas_call x0 -> x1, Pallas kernels: none -> 82.4 us  [on_device(): pl.pallas_call(functools.partial(kernel, (n_node, n_orb, nzl, ny, nx, nzh...]
    ppermute x24 -> x0, waiting for transfers between devices: 56.9 us -> none  [the longest x12 48.3 us: padded_2(): lax.ppermute(lax.slice_in_dim(block, 0, width, axis=dim), axis, backward)]
    all_to_all x3 -> x0, starting transfers between devices: 19 us -> none  [the longest x1 9.72 us: on_device(): lax.all_to_all(coeff_buf.reshape(count_node, capacity), 'node', split_axi...]
    all_to_all x3 -> x0, waiting for transfers between devices: 14.2 us -> none  [the longest x1 8.54 us: on_device(): lax.all_to_all(start_buf.reshape(count_node, capacity), 'node', split_axi...]
  transfers between devices with their start and end apart: 28 -> 0, of which waited for: 17 -> 0; matrix products, arithmetic and copies ran while one was open for 21% -> 0% of each run, Pallas kernels for 0% -> 0%
where the time goes in v1:
time: 88.1 us; the launch traced here: 87.8 us
  Pallas kernels  82.4 us (94%)
  local copies, waits for them, and re-layouts  4.73 us (5%)
    pallas_call x1, Pallas kernels, on_device(): pl.pallas_call(functools.partial(kernel, (n_node, n_orb, nzl, ny, nx, nzh...  82.4 us
    unnamed x16, local copies, waits for them, and re-layouts  4.73 us

profile of v1, /device:TPU:1, one launch (start us, length us, event | category | flops | bytes accessed | tf_op | source)
XLA Modules:
  0.0 87.8 jit_solution(13472646018070661231)
XLA Ops:
  0.6 0.0 copy-start.3
  0.6 0.0 copy-start.4
  0.7 0.0 copy-start.5
  0.7 0.0 copy-start.6
  0.7 0.6 copy-done.3
  1.3 0.0 copy-done.4
  1.3 0.0 copy-done.5
  1.3 0.0 copy-done.6
  1.3 0.0 copy-start
  1.3 1.0 %copy-done = bf16[2,4,128,256]{3,2,1,0:T(8,128)(2,1)S(1)} copy-done((bf16[2,4,128,256]{3,2,1,0:T(8,128)(2,1)S(1)}, bf16[2,4,128,256]{3,2,1,0:T(8,128)(2,1)}, u32[]{:S(2)}) %copy-start) | copy-done | bytes 524312
  2.4 0.0 copy-start.1
  2.4 0.9 %copy-done.1 = bf16[2,4,128,128]{3,2,1,0:T(8,128)(2,1)S(1)} copy-done((bf16[2,4,128,128]{3,2,1,0:T(8,128)(2,1)S(1)}, bf16[2,4,128,128]{3,2,1,0:T(8,128)(2,1)}, u32[]{:S(2)}) %copy-start.1) | copy-done | bytes 262168
  3.3 0.0 copy-start.2
  3.3 0.7 copy-done.2
  4.0 82.4 %shard_map.86 = (bf16[2,4,128,128]{3,2,1,0:T(8,128)(2,1)S(1)}, f32[128,256]{1,0:T(8,128)S(1)}) custom-call(bf16[2,4,128,128]{3,2,1,0:T(8,128)(2,1)S(1)} %copy-done.1, bf16[2,4,128,256]{3,2,1,0:T(8,128)(2,1)S(1)} %copy-done, f32[8,128]{1,0:T(8,128)S(1)} %bitcast.4, bf16[24,256]{1,0:T(8,128)(2,1)S(1)} %copy-done.2, bf16[1,24]{1,0:T(2,128)(2,1)S(1)} %bitcast.5, ...), custom_call_target="tpu_custom_call" | custom-call | tf_op jit(solution)/shard_map/pallas_call | solution.py:454
  86.5 0.7 copy.11
  87.2 0.7 copy.12
Async XLA Ops:
  0.6 0.7 copy-start.3
  0.6 0.7 copy-start.4
  0.7 0.7 copy-start.5
  0.7 0.7 copy-start.6
  1.3 1.0 %copy-start = (bf16[2,4,128,256]{3,2,1,0:T(8,128)(2,1)S(1)}, bf16[2,4,128,256]{3,2,1,0:T(8,128)(2,1)}, u32[]{:S(2)}) copy-start(bf16[2,4,128,256]{3,2,1,0:T(8,128)(2,1)} %orbit_ref.1) | copy-start | bytes 1572868
  2.4 0.9 %copy-start.1 = (bf16[2,4,128,128]{3,2,1,0:T(8,128)(2,1)S(1)}, bf16[2,4,128,128]{3,2,1,0:T(8,128)(2,1)}, u32[]{:S(2)}) copy-start(bf16[2,4,128,128]{3,2,1,0:T(8,128)(2,1)} %panel_ref.1) | copy-start | bytes 786436
  3.3 0.7 copy-start.2

commit v2 on v1

--- a/solution.py
+++ b/solution.py
@@ -27,11 +27,11 @@
     scales,
     panel_ref,
     orbit_ref,
-    pot_ref,
-    proj_ref,
-    str_ref,
-    dom_ref,
-    start_ref,
+    pot_hbm,
+    proj_hbm,
+    str_hbm,
+    dom_hbm,
+    start_hbm,
     out_ref,
     inter_ref,
     y,
@@ -41,10 +41,18 @@
     hyh,
     diag,
     orb_v,
+    pot_ref,
+    proj_ref,
+    str_ref,
+    dom_ref,
+    start_ref,
     w_ref,
     m_ref,
     apack,
+    amid,
     abuf,
+    pieces,
+    crecv,
     part,
     rs,
     ar_src,
@@ -70,13 +78,29 @@
     xx = orb // nzh
     zh = lax.rem(orb, nzh)
     n_xy = nx * ny
-    n_zc = nzh * nzl * 2
+    n_z = nzh * nzl
+    n_yc = 2 * ny
+    me_yc = lax.rem(node, n_yc)
     wx, wy, nz, cols = panel_ref.shape
     ch = nz // CHUNKS
 
     load_panel = pltpu.make_async_copy(panel_ref, y.at[0], load_sem.at[0])
     load_panel.start()
     load_orbit = pltpu.make_async_copy(orbit_ref, orb_v, load_sem.at[1])
+    loads = [
+        pltpu.make_async_copy(src, dst, load_sem.at[2 + i])
+        for i, (src, dst) in enumerate(
+            (
+                (dom_hbm, dom_ref),
+                (start_hbm, start_ref),
+                (str_hbm, str_ref),
+                (proj_hbm, proj_ref),
+                (pot_hbm, pot_ref),
+            )
+        )
+    ]
+    for load in loads:
+        load.start()
     load_orbit.start()
 
     barrier = pltpu.get_barrier_semaphore()
@@ -86,11 +110,11 @@
             barrier, inc=1, device_id=(target_node, target_orb), device_id_type=MESH
         )
 
-    def greet_node(i, carry):
-        greet(lax.rem(node + i, n_node), orb)
+    def greet_yc(i, carry):
+        greet(zl * n_yc + lax.rem(me_yc + i, n_yc), orb)
         return carry
 
-    lax.fori_loop(1, n_node, greet_node, 0)
+    lax.fori_loop(1, n_yc, greet_yc, 0)
 
     def greet_x(i, carry):
         gx = lax.rem(xx + 1 + i // ny, nx)
@@ -99,28 +123,37 @@
         return carry
 
     lax.fori_loop(0, (nx - 1) * ny, greet_x, 0)
+    me_z = zh * nzl + zl
+
+    def z_target(i):
+        g = lax.rem(me_z + i, n_z)
+        return g, ((lax.rem(g, nzl) * ny + yy) * 2 + core, xx * nzh + g // nzl)
 
     def greet_z(i, carry):
-        gz = lax.rem(zh + 1 + i // (2 * nzl), nzh)
-        rest = lax.rem(i, 2 * nzl)
-        greet(((rest // 2) * ny + yy) * 2 + lax.rem(rest, 2), xx * nzh + gz)
+        greet(*z_target(i)[1])
         return carry
 
-    lax.fori_loop(0, (nzh - 1) * 2 * nzl, greet_z, 0)
-    greeted = (n_node - 1) + (nx - 1) * ny + (nzh - 1) * 2 * nzl
+    lax.fori_loop(1, n_z, greet_z, 0)
+    greeted = (n_yc - 1) + (nx - 1) * ny + (n_z - 1)
     up_cross = jnp.logical_and(zh == nzh - 1, orb < n_orb - 1)
     down_cross = jnp.logical_and(zh == 0, orb > 0)
 
-    @pl.when(up_cross)
-    def _():
-        greet(node, orb + 1)
-
-    @pl.when(down_cross)
-    def _():
-        greet(node, orb - 1)
-
-    crossings = up_cross.astype(jnp.int32) + down_cross.astype(jnp.int32)
-    pl.semaphore_wait(barrier, greeted + crossings)
+    up_seam = jnp.logical_and(me_yc == n_yc - 1, node < n_node - 1)
+    down_seam = jnp.logical_and(me_yc == 0, node > 0)
+    for crosses, target in (
+        (up_cross, (node, orb + 1)),
+        (down_cross, (node, orb - 1)),
+        (up_seam, (node + 1, orb)),
+        (down_seam, (node - 1, orb)),
+    ):
+
+        @pl.when(crosses)
+        def _(target=target):
+            greet(*target)
+
+        greeted = greeted + crosses.astype(jnp.int32)
+
+    pl.semaphore_wait(barrier, greeted)
 
     def halo(side, k, c):
         zs = pl.ds(c * ch, ch)
@@ -144,8 +177,8 @@
     sends = (node < n_node - 1, node > 0, orb < n_orb - 1, orb > 0)
     receives = (node > 0, node < n_node - 1, orb > 0, orb < n_orb - 1)
 
-    def send_halo(k, c):
-        for side in (2, 3, 0, 1):
+    def send_halo(k, c, which):
+        for side in which:
 
             @pl.when(sends[side])
             def _(side=side):
@@ -160,7 +193,9 @@
 
     load_panel.wait()
     for c in range(CHUNKS):
-        send_halo(0, c)
+        send_halo(0, c, (2, 3))
+    for c in range(CHUNKS):
+        send_halo(0, c, (0, 1))
 
     for side, buf in enumerate((hxl, hxh, hyl, hyh)):
 
@@ -173,6 +208,8 @@
             lax.fori_loop(0, DEG, clear, 0)
 
     atoms = proj_ref.shape[0]
+    for load in loads:
+        load.wait()
     f32 = jnp.float32
     a_sub = lax.broadcasted_iota(jnp.int32, (atoms, atoms), 0)
     a_lane = lax.broadcasted_iota(jnp.int32, (atoms, atoms), 1)
@@ -212,25 +249,40 @@
         choose = jnp.where(jnp.logical_and(named, slot_row == code), 1.0, 0.0)
         term = jnp.dot(choose, piece, preferred_element_type=f32)
         packed = term if packed is None else packed + term
-    apack[...] = packed.reshape(n_node, 8, 128)
-
-    def atom_copy(i):
-        other = lax.rem(node + i, n_node)
-        return pltpu.make_async_remote_copy(
-            src_ref=apack.at[other],
-            dst_ref=abuf.at[node],
-            send_sem=asend,
-            recv_sem=arecv,
-            device_id=(other, orb),
+    apack[...] = packed.reshape(nzl, n_yc, 8, 128)
+
+    def send_atoms(i, carry):
+        other = lax.rem(me_yc + i, n_yc)
+        pltpu.make_async_remote_copy(
+            src_ref=apack.at[:, other],
+            dst_ref=amid.at[:, me_yc],
+            send_sem=asend.at[0],
+            recv_sem=arecv.at[0],
+            device_id=(zl * n_yc + other, orb),
             device_id_type=MESH,
-        )
-
-    def send_atoms(i, carry):
-        atom_copy(i).start()
+        ).start()
         return carry
 
-    lax.fori_loop(1, n_node, send_atoms, 0)
-    abuf[node] = apack[node]
+    lax.fori_loop(1, n_yc, send_atoms, 0)
+    amid[:, me_yc] = apack[:, me_yc]
+
+    first_moved = pltpu.make_async_remote_copy(
+        src_ref=amid.at[:, pl.ds(0, n_yc - 1)],
+        dst_ref=amid.at[:, pl.ds(0, n_yc - 1)],
+        send_sem=asend.at[0],
+        recv_sem=arecv.at[0],
+        device_id=(node + 1 - 2 * core, orb),
+        device_id_type=MESH,
+    )
+    if nzl > 1:
+        second_moved = pltpu.make_async_remote_copy(
+            src_ref=abuf.at[pl.ds(0, nzl - 1)],
+            dst_ref=abuf.at[pl.ds(0, nzl - 1)],
+            send_sem=asend.at[1],
+            recv_sem=arecv.at[1],
+            device_id=(node + 1 - 2 * core, orb),
+            device_id_type=MESH,
+        )
 
     for ix in range(wx):
         for iy in range(wy):
@@ -267,39 +319,49 @@
                     )
                 base.append(line)
             wait_halo(k, c)
-            for ix in range(wx):
-                for iy in range(wy):
-                    side = (hxl if ix == 0 else hxh)[k, iy, zs].astype(f32)
-                    if iy == 0:
-                        side = side + hyl[k, ix, zs].astype(f32)
-                    if iy == wy - 1:
-                        side = side + hyh[k, ix, zs].astype(f32)
-                    y[k + 1, ix, iy, zs] = (base[ix][iy] - arm * side).astype(jnp.bfloat16)
-
-            @pl.when(k < DEG - 1)
-            def _():
-                send_halo(lax.min(k + 1, DEG - 1), c)
+            for lines, which in (((0, wy - 1), (2, 3)), (range(1, wy - 1), (0, 1))):
+                for iy in lines:
+                    for ix in range(wx):
+                        side = (hxl if ix == 0 else hxh)[k, iy, zs].astype(f32)
+                        if iy == 0:
+                            side = side + hyl[k, ix, zs].astype(f32)
+                        if iy == wy - 1:
+                            side = side + hyh[k, ix, zs].astype(f32)
+                        y[k + 1, ix, iy, zs] = (base[ix][iy] - arm * side).astype(jnp.bfloat16)
+
+                @pl.when(k < DEG - 1)
+                def _(which=which, c=c):
+                    send_halo(lax.min(k + 1, DEG - 1), c, which)
 
         return carry
 
-    lax.fori_loop(0, DEG // 2, step, 0)
-
-    pltpu.make_async_remote_copy(
-        src_ref=abuf.at[pl.ds(0, n_node - 1)],
-        dst_ref=abuf.at[pl.ds(0, n_node - 1)],
-        send_sem=asend,
-        recv_sem=arecv,
-        device_id=(lax.rem(node + 1, n_node), orb),
-        device_id_type=MESH,
-    ).wait_recv()
+    lax.fori_loop(0, 2, step, 0)
+
+    first_moved.wait_recv()
+    for ahead in range(1, nzl):
+        other = lax.rem(zl + ahead, nzl)
+        pltpu.make_async_remote_copy(
+            src_ref=amid.at[other],
+            dst_ref=abuf.at[zl],
+            send_sem=asend.at[1],
+            recv_sem=arecv.at[1],
+            device_id=(other * n_yc + me_yc, orb),
+            device_id_type=MESH,
+        ).start()
+    abuf[zl] = amid[zl]
+
+    lax.fori_loop(2, 4, step, 0)
+
+    if nzl > 1:
+        second_moved.wait_recv()
     load_orbit.wait()
     blocks = wx * wy
     s_lane = lax.broadcasted_iota(jnp.int32, (n_node, 128), 1).astype(f32)
     coeffs = []
     for slot in range(2):
-        v0 = abuf[:, 2 * slot, :]
-        v1 = abuf[:, 2 * slot + 1, :]
-        info = abuf[:, 4 + slot, :]
+        v0 = abuf[:, :, 2 * slot, :].reshape(n_node, 128)
+        v1 = abuf[:, :, 2 * slot + 1, :].reshape(n_node, 128)
+        info = abuf[:, :, 4 + slot, :].reshape(n_node, 128)
         lo, hi, coeff = info[:, 0:1], info[:, 1:2], info[:, 2:3]
         inside = s_lane >= lo
         placed = (
@@ -335,7 +397,7 @@
         m_ref[j * 128 : (j + 1) * 128, :norb] = whole_hi
         m_ref[j * 128 : (j + 1) * 128, norb:] = (whole - whole_hi.astype(f32)).astype(jnp.bfloat16)
 
-    lax.fori_loop(DEG // 2, DEG, step, 0)
+    lax.fori_loop(4, DEG, step, 0)
 
     save = pltpu.make_async_copy(y.at[DEG], out_ref, out_sem)
     save.start()
@@ -349,23 +411,19 @@
     wide = norb // 128
     tiles = (cols // 8) * wide
     per = tiles // n_xy
+
     for t in range(tiles):
-        part[t // per, (t % per) * 8 : (t % per + 1) * 8, :] = share[
-            (t // wide) * 8 : (t // wide + 1) * 8, (t % wide) * 128 : (t % wide + 1) * 128
-        ]
-
+        for half in range(2):
+            row = (t // wide) * 8 + half * 4
+            pieces[half, t // per, (t % per) * 4 : (t % per + 1) * 4, :] = share[
+                row : row + 4, (t % wide) * 128 : (t % wide + 1) * 128
+            ]
     me_xy = xx * ny + yy
-    me_zc = (zh * nzl + zl) * 2 + core
+    across = (node + 1 - 2 * core, orb)
 
     def plane_target(i):
         g = lax.rem(me_xy + i, n_xy)
-        gy = lax.rem(g, ny)
-        return g, ((zl * ny + gy) * 2 + core, (g // ny) * nzh + zh)
-
-    def line_target(i):
-        g = lax.rem(me_zc + i, n_zc)
-        gz = g // 2
-        return g, ((lax.rem(gz, nzl) * ny + yy) * 2 + lax.rem(g, 2), xx * nzh + gz // nzl)
+        return g, ((zl * ny + lax.rem(g, ny)) * 2 + core, (g // ny) * nzh + zh)
 
     def exchange(stage, count, target_of, source_of, dst, mine):
         def send(i, carry):
@@ -382,33 +440,53 @@
 
         lax.fori_loop(1, count, send, 0)
 
-    def arrived(stage, count, target_of, dst):
-        pltpu.make_async_remote_copy(
-            src_ref=dst.at[pl.ds(0, count - 1)],
-            dst_ref=dst.at[pl.ds(0, count - 1)],
+    def moved(stage, ref):
+        return pltpu.make_async_remote_copy(
+            src_ref=ref,
+            dst_ref=ref,
             send_sem=rsend.at[stage],
             recv_sem=rrecv.at[stage],
-            device_id=target_of(1)[1],
+            device_id=across,
             device_id_type=MESH,
-        ).wait()
-
-    exchange(0, n_xy, plane_target, lambda g: part.at[g], rs, me_xy)
+        )
+
+    def to_core(stage, src, dst):
+        return pltpu.make_async_remote_copy(
+            src_ref=src,
+            dst_ref=dst,
+            send_sem=rsend.at[stage],
+            recv_sem=rrecv.at[stage],
+            device_id=across,
+            device_id_type=MESH,
+        )
+
+    swap = to_core(0, pieces.at[1 - core], crecv)
+    swap.start()
+    swap.wait_recv()
+    part[...] = pieces[core] + crecv[...]
+    exchange(1, n_xy, plane_target, lambda g: part.at[g], rs, me_xy)
     rs[me_xy] = part[me_xy]
-    arrived(0, n_xy, plane_target, rs)
+    moved(1, rs.at[pl.ds(0, n_xy - 1)]).wait_recv()
     own = jnp.sum(rs[...], axis=0)
     ar_src[...] = own
-    exchange(1, n_zc, line_target, lambda g: ar_src, ar, me_zc)
-    ar[me_zc] = own
-    arrived(1, n_zc, line_target, ar)
+    exchange(2, n_z, z_target, lambda g: ar_src, ar, me_z)
+    ar[me_z] = own
+    moved(2, ar.at[pl.ds(0, n_z - 1)]).wait_recv()
     own = jnp.sum(ar[...], axis=0)
     ag_src[...] = own
-    exchange(2, n_xy, plane_target, lambda g: ag_src, ag, me_xy)
-    ag[me_xy] = own
-    arrived(2, n_xy, plane_target, ag)
+    mine = ag.at[core]
+    exchange(3, n_xy, plane_target, lambda g: ag_src, mine, me_xy)
+    ag[core, me_xy] = own
+    moved(3, mine.at[pl.ds(0, n_xy - 1)]).wait_recv()
+    back = to_core(4, mine, mine)
+    back.start()
+    back.wait_recv()
     for t in range(tiles):
-        inter_ref[
-            (t // wide) * 8 : (t // wide + 1) * 8, (t % wide) * 128 : (t % wide + 1) * 128
-        ] = ag[t // per, (t % per) * 8 : (t % per + 1) * 8, :]
+        for half in range(2):
+            row = (t // wide) * 8 + half * 4
+            inter_ref[row : row + 4, (t % wide) * 128 : (t % wide + 1) * 128] = ag[
+                half, t // per, (t % per) * 4 : (t % per + 1) * 4, :
+            ]
 
     for side, buf in enumerate((hxl, hxh, hyl, hyh)):
 
@@ -423,14 +501,14 @@
                 device_id_type=MESH,
             ).wait_send()
 
-    pltpu.make_async_remote_copy(
-        src_ref=abuf.at[pl.ds(0, n_node - 1)],
-        dst_ref=abuf.at[pl.ds(0, n_node - 1)],
-        send_sem=asend,
-        recv_sem=arecv,
-        device_id=(lax.rem(node + 1, n_node), orb),
-        device_id_type=MESH,
-    ).wait_send()
+    swap.wait_send()
+    moved(1, rs.at[pl.ds(0, n_xy - 1)]).wait_send()
+    moved(2, ar.at[pl.ds(0, n_z - 1)]).wait_send()
+    moved(3, mine.at[pl.ds(0, n_xy - 1)]).wait_send()
+    back.wait_send()
+    first_moved.wait_send()
+    if nzl > 1:
+        second_moved.wait_send()
     save.wait()
 
 
@@ -440,16 +518,16 @@
     n_node = lax.axis_size("node")
     n_orb = lax.axis_size("orb")
     nzl, ny, nx, nzh = factors(n_node, n_orb)
-    n_xy, n_zc = nx * ny, nzh * nzl * 2
+    n_xy, n_z = nx * ny, nzh * nzl
     atoms = projectors.shape[0]
     nodes_all = n_node * wx * n_orb * wy * nz
     atoms_all = atoms * n_node * n_orb
     c1 = 1.0 / math.sqrt(nodes_all)
     ratio = math.sqrt(nodes_all) / math.sqrt(atoms_all)
-    rows = (cols // 8) * (norb // 128) // n_xy * 8
+    rows = (cols // 8) * (norb // 128) // n_xy * 4
     bf16, f32 = jnp.bfloat16, jnp.float32
     vmem = pl.BlockSpec(memory_space=pltpu.VMEM)
-    hbm = pl.BlockSpec(memory_space=pl.ANY)
+    hbm = pl.BlockSpec(memory_space=pltpu.HBM)
     dma = pltpu.SemaphoreType.DMA
     return pl.pallas_call(
         functools.partial(kernel, (n_node, n_orb, nzl, ny, nx, nzh), (c1, ratio)),
@@ -457,7 +535,7 @@
             jax.ShapeDtypeStruct(panel.shape, bf16),
             jax.ShapeDtypeStruct((cols, norb), f32),
         ),
-        in_specs=[hbm, hbm] + [vmem] * 5,
+        in_specs=[hbm] * 7,
         out_specs=(hbm, vmem),
         scratch_shapes=[
             pltpu.VMEM((DEG + 1, wx, wy, nz, cols), bf16),
@@ -467,27 +545,35 @@
             pltpu.VMEM((DEG, wx, nz, cols), bf16),
             pltpu.VMEM((wx, wy, nz, cols), f32),
             pltpu.VMEM((wx, wy, nz, norb), bf16),
+            pltpu.VMEM((wx * wy, nz), f32),
+            pltpu.VMEM(projectors.shape, bf16),
+            pltpu.VMEM((1, atoms), bf16),
+            pltpu.VMEM((1, atoms), jnp.int32),
+            pltpu.VMEM((1, atoms), jnp.int32),
             pltpu.VMEM((2 * n_node, wx * wy * nz), bf16),
             pltpu.VMEM((wx * wy * nz, 2 * norb), bf16),
-            pltpu.VMEM((n_node, 8, 128), f32),
-            pltpu.VMEM((n_node, 8, 128), f32),
+            pltpu.VMEM((nzl, 2 * ny, 8, 128), f32),
+            pltpu.VMEM((nzl, 2 * ny, 8, 128), f32),
+            pltpu.VMEM((nzl, 2 * ny, 8, 128), f32),
+            pltpu.VMEM((2, n_xy, rows, 128), f32),
+            pltpu.VMEM((n_xy, rows, 128), f32),
             pltpu.VMEM((n_xy, rows, 128), f32),
             pltpu.VMEM((n_xy, rows, 128), f32),
             pltpu.VMEM((rows, 128), f32),
-            pltpu.VMEM((n_zc, rows, 128), f32),
+            pltpu.VMEM((n_z, rows, 128), f32),
             pltpu.VMEM((rows, 128), f32),
-            pltpu.VMEM((n_xy, rows, 128), f32),
-            dma((2,)),
+            pltpu.VMEM((2, n_xy, rows, 128), f32),
+            dma((7,)),
             dma,
             dma((4,)),
             dma((DEG, 4, CHUNKS)),
-            dma,
-            dma,
-            dma((3,)),
-            dma((3,)),
+            dma((2,)),
+            dma((2,)),
+            dma((5,)),
+            dma((5,)),
         ],
         compiler_params=pltpu.CompilerParams(
-            collective_id=0, has_side_effects=True, vmem_limit_bytes=48 * 1024 * 1024
+            collective_id=0, has_side_effects=True, vmem_limit_bytes=63 * 1024 * 1024
         ),
     )(
         panel,

time: 88.1 us -> 86.5 us (0.982)
  local copies, waits for them, and re-layouts: 4.73 us -> 2.37 us
  Pallas kernels: 82.4 us -> 83.3 us
    unnamed x16 -> x4, local copies, waits for them, and re-layouts: 4.73 us -> 2.37 us
    pallas_call x1, Pallas kernels: 82.4 us -> 83.3 us  [on_device(): pl.pallas_call(functools.partial(kernel, (n_node, n_orb, nzl, ny, nx, nzh...]
where the time goes in v2:
time: 86.5 us; the launch traced here: 86.3 us
  Pallas kernels  83.3 us (96%)
  local copies, waits for them, and re-layouts  2.37 us (3%)
    pallas_call x1, Pallas kernels, on_device(): pl.pallas_call(functools.partial(kernel, (n_node, n_orb, nzl, ny, nx, nzh...  83.3 us
    unnamed x4, local copies, waits for them, and re-layouts  2.37 us

profile of v2, /device:TPU:1, one launch (start us, length us, event | category | flops | bytes accessed | tf_op | source)
XLA Modules:
  0.0 86.3 jit_solution(18168111675132512077)
XLA Ops:
  0.6 83.3 %shard_map.86 = (bf16[2,4,128,128]{3,2,1,0:T(8,128)(2,1)}, f32[128,256]{1,0:T(8,128)}) custom-call(bf16[2,4,128,128]{3,2,1,0:T(8,128)(2,1)} %panel_ref.1, bf16[2,4,128,256]{3,2,1,0:T(8,128)(2,1)} %orbit_ref.1, f32[8,128]{1,0:T(8,128)} %bitcast.4, bf16[24,256]{1,0:T(8,128)(2,1)} %proj_hbm.1, bf16[1,24]{1,0:T(2,128)(2,1)} %bitcast.5, s32[1,24]{1,0:T(1,128)} %bitcast.6, ...), custom_call_target="tpu_custom_call" | custom-call | tf_op jit(solution)/shard_map/pallas_call | solution.py:532
  84.0 0.0 copy-start
  84.0 1.7 %copy.11 = bf16[2,4,128,128]{3,2,1,0:T(8,128)(2,1)} copy(bf16[2,4,128,128]{3,2,1,0:T(8,128)(2,1)} %get-tuple-element.4) | data formatting | bytes 524288
  85.7 0.0 copy-done
  85.7 0.7 copy.12
Async XLA Ops:
  84.0 1.7 %copy-start = (f32[128,256]{1,0:T(8,128)S(1)}, f32[128,256]{1,0:T(8,128)}, u32[]{:S(2)}) copy-start(f32[128,256]{1,0:T(8,128)} %get-tuple-element.5) | copy-start | bytes 393220

commit v3 on v2

--- a/solution.py
+++ b/solution.py
@@ -52,7 +52,6 @@
     amid,
     abuf,
     pieces,
-    crecv,
     part,
     rs,
     ar_src,
@@ -413,11 +412,9 @@
     per = tiles // n_xy
 
     for t in range(tiles):
-        for half in range(2):
-            row = (t // wide) * 8 + half * 4
-            pieces[half, t // per, (t % per) * 4 : (t % per + 1) * 4, :] = share[
-                row : row + 4, (t % wide) * 128 : (t % wide + 1) * 128
-            ]
+        part[t // per, (t % per) * 8 : (t % per + 1) * 8, :] = share[
+            (t // wide) * 8 : (t // wide + 1) * 8, (t % wide) * 128 : (t % wide + 1) * 128
+        ]
     me_xy = xx * ny + yy
     across = (node + 1 - 2 * core, orb)
 
@@ -460,33 +457,28 @@
             device_id_type=MESH,
         )
 
-    swap = to_core(0, pieces.at[1 - core], crecv)
-    swap.start()
-    swap.wait_recv()
-    part[...] = pieces[core] + crecv[...]
     exchange(1, n_xy, plane_target, lambda g: part.at[g], rs, me_xy)
     rs[me_xy] = part[me_xy]
     moved(1, rs.at[pl.ds(0, n_xy - 1)]).wait_recv()
     own = jnp.sum(rs[...], axis=0)
+    pieces[core] = own
+    swap = to_core(0, pieces.at[core], pieces.at[core])
+    swap.start()
+    swap.wait_recv()
+    own = pieces[0] + pieces[1]
     ar_src[...] = own
     exchange(2, n_z, z_target, lambda g: ar_src, ar, me_z)
     ar[me_z] = own
     moved(2, ar.at[pl.ds(0, n_z - 1)]).wait_recv()
     own = jnp.sum(ar[...], axis=0)
     ag_src[...] = own
-    mine = ag.at[core]
-    exchange(3, n_xy, plane_target, lambda g: ag_src, mine, me_xy)
-    ag[core, me_xy] = own
-    moved(3, mine.at[pl.ds(0, n_xy - 1)]).wait_recv()
-    back = to_core(4, mine, mine)
-    back.start()
-    back.wait_recv()
+    exchange(3, n_xy, plane_target, lambda g: ag_src, ag, me_xy)
+    ag[me_xy] = own
+    moved(3, ag.at[pl.ds(0, n_xy - 1)]).wait_recv()
     for t in range(tiles):
-        for half in range(2):
-            row = (t // wide) * 8 + half * 4
-            inter_ref[row : row + 4, (t % wide) * 128 : (t % wide + 1) * 128] = ag[
-                half, t // per, (t % per) * 4 : (t % per + 1) * 4, :
-            ]
+        inter_ref[
+            (t // wide) * 8 : (t // wide + 1) * 8, (t % wide) * 128 : (t % wide + 1) * 128
+        ] = ag[t // per, (t % per) * 8 : (t % per + 1) * 8, :]
 
     for side, buf in enumerate((hxl, hxh, hyl, hyh)):
 
@@ -504,8 +496,7 @@
     swap.wait_send()
     moved(1, rs.at[pl.ds(0, n_xy - 1)]).wait_send()
     moved(2, ar.at[pl.ds(0, n_z - 1)]).wait_send()
-    moved(3, mine.at[pl.ds(0, n_xy - 1)]).wait_send()
-    back.wait_send()
+    moved(3, ag.at[pl.ds(0, n_xy - 1)]).wait_send()
     first_moved.wait_send()
     if nzl > 1:
         second_moved.wait_send()
@@ -524,7 +515,7 @@
     atoms_all = atoms * n_node * n_orb
     c1 = 1.0 / math.sqrt(nodes_all)
     ratio = math.sqrt(nodes_all) / math.sqrt(atoms_all)
-    rows = (cols // 8) * (norb // 128) // n_xy * 4
+    rows = (cols // 8) * (norb // 128) // n_xy * 8
     bf16, f32 = jnp.bfloat16, jnp.float32
     vmem = pl.BlockSpec(memory_space=pltpu.VMEM)
     hbm = pl.BlockSpec(memory_space=pltpu.HBM)
@@ -555,14 +546,13 @@
             pltpu.VMEM((nzl, 2 * ny, 8, 128), f32),
             pltpu.VMEM((nzl, 2 * ny, 8, 128), f32),
             pltpu.VMEM((nzl, 2 * ny, 8, 128), f32),
-            pltpu.VMEM((2, n_xy, rows, 128), f32),
-            pltpu.VMEM((n_xy, rows, 128), f32),
+            pltpu.VMEM((2, rows, 128), f32),
             pltpu.VMEM((n_xy, rows, 128), f32),
             pltpu.VMEM((n_xy, rows, 128), f32),
             pltpu.VMEM((rows, 128), f32),
             pltpu.VMEM((n_z, rows, 128), f32),
             pltpu.VMEM((rows, 128), f32),
-            pltpu.VMEM((2, n_xy, rows, 128), f32),
+            pltpu.VMEM((n_xy, rows, 128), f32),
             dma((7,)),
             dma,
             dma((4,)),

time: 86.5 us -> 85.2 us (0.985)
  Pallas kernels: 83.3 us -> 82 us
    pallas_call x1, Pallas kernels: 83.3 us -> 82 us  [on_device(): pl.pallas_call(functools.partial(kernel, (n_node, n_orb, nzl, ny, nx, nzh...]
where the time goes in v3:
time: 85.2 us; the launch traced here: 85 us
  Pallas kernels  82 us (96%)
  local copies, waits for them, and re-layouts  2.37 us (3%)
    pallas_call x1, Pallas kernels, on_device(): pl.pallas_call(functools.partial(kernel, (n_node, n_orb, nzl, ny, nx, nzh...  82 us
    unnamed x4, local copies, waits for them, and re-layouts  2.37 us

profile of v3, /device:TPU:1, one launch (start us, length us, event | category | flops | bytes accessed | tf_op | source)
XLA Modules:
  0.0 85.0 jit_solution(2779687830783981892)
XLA Ops:
  0.6 82.0 %shard_map.86 = (bf16[2,4,128,128]{3,2,1,0:T(8,128)(2,1)}, f32[128,256]{1,0:T(8,128)}) custom-call(bf16[2,4,128,128]{3,2,1,0:T(8,128)(2,1)} %panel_ref.1, bf16[2,4,128,256]{3,2,1,0:T(8,128)(2,1)} %orbit_ref.1, f32[8,128]{1,0:T(8,128)} %bitcast.4, bf16[24,256]{1,0:T(8,128)(2,1)} %proj_hbm.1, bf16[1,24]{1,0:T(2,128)(2,1)} %bitcast.5, s32[1,24]{1,0:T(1,128)} %bitcast.6, ...), custom_call_target="tpu_custom_call" | custom-call | tf_op jit(solution)/shard_map/pallas_call | solution.py:523
  82.7 0.0 copy-start
  82.7 1.7 %copy.11 = bf16[2,4,128,128]{3,2,1,0:T(8,128)(2,1)} copy(bf16[2,4,128,128]{3,2,1,0:T(8,128)(2,1)} %get-tuple-element.4) | data formatting | bytes 524288
  84.4 0.0 copy-done
  84.4 0.7 copy.12
Async XLA Ops:
  82.7 1.7 %copy-start = (f32[128,256]{1,0:T(8,128)S(1)}, f32[128,256]{1,0:T(8,128)}, u32[]{:S(2)}) copy-start(f32[128,256]{1,0:T(8,128)} %get-tuple-element.5) | copy-start | bytes 393220

commit v4 on v3

--- a/solution.py
+++ b/solution.py
@@ -125,7 +125,9 @@
     me_z = zh * nzl + zl
 
     def z_target(i):
-        g = lax.rem(me_z + i, n_z)
+        step = i // 2
+        step = jnp.where(lax.rem(i, 2) == 0, step, -step)
+        g = lax.rem(me_z + n_z // 2 + step + n_z, n_z)
         return g, ((lax.rem(g, nzl) * ny + yy) * 2 + core, xx * nzh + g // nzl)
 
     def greet_z(i, carry):
@@ -192,9 +194,7 @@
 
     load_panel.wait()
     for c in range(CHUNKS):
-        send_halo(0, c, (2, 3))
-    for c in range(CHUNKS):
-        send_halo(0, c, (0, 1))
+        send_halo(0, c, (2, 3, 0, 1))
 
     for side, buf in enumerate((hxl, hxh, hyl, hyh)):
 
@@ -419,7 +419,11 @@
     across = (node + 1 - 2 * core, orb)
 
     def plane_target(i):
-        g = lax.rem(me_xy + i, n_xy)
+        i = i - 1
+        dx, dy = i // ny, lax.rem(i, ny)
+        dx = nx // 2 + jnp.where(lax.rem(dx, 2) == 0, dx // 2, -((dx + 1) // 2))
+        dy = ny // 2 + jnp.where(lax.rem(dy, 2) == 0, dy // 2, -((dy + 1) // 2))
+        g = lax.rem(xx + dx, nx) * ny + lax.rem(yy + dy, ny)
         return g, ((zl * ny + lax.rem(g, ny)) * 2 + core, (g // ny) * nzh + zh)
 
     def exchange(stage, count, target_of, source_of, dst, mine):

time: 85.2 us -> 84.9 us (level)
  no operation moved by 1% of the time
where the time goes in v4:
time: 84.9 us; the launch traced here: 84.8 us
  Pallas kernels  81.8 us (96%)
  local copies, waits for them, and re-layouts  2.37 us (3%)
    pallas_call x1, Pallas kernels, on_device(): pl.pallas_call(functools.partial(kernel, (n_node, n_orb, nzl, ny, nx, nzh...  81.8 us
    unnamed x4, local copies, waits for them, and re-layouts  2.37 us

profile of v4, /device:TPU:1, one launch (start us, length us, event | category | flops | bytes accessed | tf_op | source)
XLA Modules:
  0.0 84.8 jit_solution(15406411008076920697)
XLA Ops:
  0.6 81.8 %shard_map.86 = (bf16[2,4,128,128]{3,2,1,0:T(8,128)(2,1)}, f32[128,256]{1,0:T(8,128)}) custom-call(bf16[2,4,128,128]{3,2,1,0:T(8,128)(2,1)} %panel_ref.1, bf16[2,4,128,256]{3,2,1,0:T(8,128)(2,1)} %orbit_ref.1, f32[8,128]{1,0:T(8,128)} %bitcast.4, bf16[24,256]{1,0:T(8,128)(2,1)} %proj_hbm.1, bf16[1,24]{1,0:T(2,128)(2,1)} %bitcast.5, s32[1,24]{1,0:T(1,128)} %bitcast.6, ...), custom_call_target="tpu_custom_call" | custom-call | tf_op jit(solution)/shard_map/pallas_call | solution.py:527
  82.4 0.0 copy-start
  82.4 1.7 %copy.11 = bf16[2,4,128,128]{3,2,1,0:T(8,128)(2,1)} copy(bf16[2,4,128,128]{3,2,1,0:T(8,128)(2,1)} %get-tuple-element.4) | data formatting | bytes 524288
  84.1 0.0 copy-done
  84.1 0.7 copy.12
Async XLA Ops:
  82.4 1.7 %copy-start = (f32[128,256]{1,0:T(8,128)S(1)}, f32[128,256]{1,0:T(8,128)}, u32[]{:S(2)}) copy-start(f32[128,256]{1,0:T(8,128)} %get-tuple-element.5) | copy-start | bytes 393220

commit v5 on v4

--- a/solution.py
+++ b/solution.py
@@ -113,7 +113,6 @@
         greet(zl * n_yc + lax.rem(me_yc + i, n_yc), orb)
         return carry
 
-    lax.fori_loop(1, n_yc, greet_yc, 0)
 
     def greet_x(i, carry):
         gx = lax.rem(xx + 1 + i // ny, nx)
@@ -121,7 +120,6 @@
         greet((zl * ny + gy) * 2 + core, gx * nzh + zh)
         return carry
 
-    lax.fori_loop(0, (nx - 1) * ny, greet_x, 0)
     me_z = zh * nzl + zl
 
     def z_target(i):
@@ -135,6 +133,8 @@
         return carry
 
     lax.fori_loop(1, n_z, greet_z, 0)
+    lax.fori_loop(0, (nx - 1) * ny, greet_x, 0)
+    lax.fori_loop(1, n_yc, greet_yc, 0)
     greeted = (n_yc - 1) + (nx - 1) * ny + (n_z - 1)
     up_cross = jnp.logical_and(zh == nzh - 1, orb < n_orb - 1)
     down_cross = jnp.logical_and(zh == 0, orb > 0)

time: 84.9 us -> 84.5 us (level)
  no operation moved by 1% of the time
where the time goes in v5:
time: 84.5 us; the launch traced here: 84.4 us
  Pallas kernels  81.4 us (96%)
  local copies, waits for them, and re-layouts  2.37 us (3%)
    pallas_call x1, Pallas kernels, on_device(): pl.pallas_call(functools.partial(kernel, (n_node, n_orb, nzl, ny, nx, nzh...  81.4 us
    unnamed x4, local copies, waits for them, and re-layouts  2.37 us

profile of v5, /device:TPU:1, one launch (start us, length us, event | category | flops | bytes accessed | tf_op | source)
XLA Modules:
  0.0 84.4 jit_solution(827743603558827307)
XLA Ops:
  0.6 81.4 %shard_map.86 = (bf16[2,4,128,128]{3,2,1,0:T(8,128)(2,1)}, f32[128,256]{1,0:T(8,128)}) custom-call(bf16[2,4,128,128]{3,2,1,0:T(8,128)(2,1)} %panel_ref.1, bf16[2,4,128,256]{3,2,1,0:T(8,128)(2,1)} %orbit_ref.1, f32[8,128]{1,0:T(8,128)} %bitcast.4, bf16[24,256]{1,0:T(8,128)(2,1)} %proj_hbm.1, bf16[1,24]{1,0:T(2,128)(2,1)} %bitcast.5, s32[1,24]{1,0:T(1,128)} %bitcast.6, ...), custom_call_target="tpu_custom_call" | custom-call | tf_op jit(solution)/shard_map/pallas_call | solution.py:527
  82.0 0.0 copy-start
  82.0 1.7 %copy.11 = bf16[2,4,128,128]{3,2,1,0:T(8,128)(2,1)} copy(bf16[2,4,128,128]{3,2,1,0:T(8,128)(2,1)} %get-tuple-element.4) | data formatting | bytes 524288
  83.7 0.0 copy-done
  83.7 0.7 copy.12
Async XLA Ops:
  82.0 1.7 %copy-start = (f32[128,256]{1,0:T(8,128)S(1)}, f32[128,256]{1,0:T(8,128)}, u32[]{:S(2)}) copy-start(f32[128,256]{1,0:T(8,128)} %get-tuple-element.5) | copy-start | bytes 393220
